TPU v7x, 32 devices: a whole 2x2x4 slice. The times are simulated.
32 devices in a mesh: groups: 1, tm: 8 (over z, core), dp: 4 (over y, x).
Axes of the slice: x: 2, y: 2, z: 4, core: 2. Of those that a mesh axis runs over, the one named last changes fastest.
Arguments:
- queries: bfloat16 [4, 2048, 1024], P(('groups', 'dp'), 'tm'), may hold values from -6.4 to 6.4
- keys: bfloat16 [4, 2048, 1024], P(('groups', 'dp'), 'tm'), may hold values from -8.8 to 8.8
- values: bfloat16 [4, 2048, 1024], P(('groups', 'dp'), 'tm'), may hold values from -6 to 6
- lengths: int32 [4], P(('groups', 'dp')), may hold values from 128 to 2048, as said below
- out_weight: bfloat16 [1024, 1024], P('dp'), may hold values from -0.1875 to 0.1875
- grad_out: bfloat16 [4, 2048, 1024], P(('groups', 'dp'), 'tm'), may hold values from -6 to 6
Outputs:
- attended: bfloat16 [4, 2048, 1024], P(('groups', 'dp'), 'tm')
- grad_queries: bfloat16 [4, 2048, 1024], P(('groups', 'dp'), 'tm')
- grad_keys: bfloat16 [4, 2048, 1024], P(('groups', 'dp'), 'tm')
- grad_values: bfloat16 [4, 2048, 1024], P(('groups', 'dp'), 'tm')
- grad_weight: float32 [1024, 1024], P(('groups', 'dp'))
Inputs may be any that keep to these rules, and one draw needn't show every extreme that they name: `lengths`: in every draw one utterance of a part fills all 2048 frames and another has exactly 128 valid frames.
All inputs are finite; a program needn't handle non-finite values.
Results may differ from a plain program's by a relative error of at most 0.0069.
Values may be sent and summed in bfloat16 or wider, within the bound.
A program may use at most 128 MiB of HBM per device.

v0:
```python
import math

import jax
import jax.numpy as jnp
from jax import lax
from jax.sharding import PartitionSpec as P

H = 8
WIN = 128


NEG_FILL = -1000000000.0


def padded(block, sides, width):
    for axis, dim in sides:
        count = lax.axis_size(axis)
        forward = [(i, i + 1) for i in range(count - 1)]
        backward = [(target, source) for source, target in forward]
        low = lax.ppermute(
            lax.slice_in_dim(block, block.shape[dim] - width, None, axis=dim), axis, forward
        )
        high = lax.ppermute(lax.slice_in_dim(block, 0, width, axis=dim), axis, backward)
        block = jnp.concatenate([low, block, high], axis=dim)
    return block


def split_heads(array, head_count):
    return array.reshape(array.shape[0], head_count, array.shape[1] // head_count)


def window_mask(query_pos, key_pos, length, reach):
    near = jnp.abs(query_pos[:, None] - key_pos[None, :]) <= reach
    live_keys = (key_pos[None, :] >= 0) & (key_pos[None, :] < length)
    live_rows = (query_pos[:, None] >= 0) & (query_pos[:, None] < length)
    return near & live_keys & live_rows


def normalize(scores, allowed):
    masked = jnp.where(allowed[None], scores, NEG_FILL)
    top = jnp.max(masked, axis=-1, keepdims=True)
    total = jnp.sum(jnp.exp(masked - top), axis=-1, keepdims=True)
    log_total = top + jnp.log(total)
    probs_f = jnp.exp(jnp.where(allowed[None], scores - log_total, NEG_FILL))
    return (log_total[..., 0], probs_f)


def per_device(queries, keys, values, lengths, out_weight, grad_out):
    tm_size = lax.axis_size("tm")
    dp_size = lax.axis_size("dp")
    rows = queries.shape[1]
    width = queries.shape[2]
    reach = WIN
    scale = 1.0 / math.sqrt(width // H)
    inv_count = 1.0 / math.sqrt(dp_size * rows * tm_size)
    length = lengths[0]
    start = lax.axis_index("tm") * rows
    query_pos = start + jnp.arange(rows, dtype=jnp.int32)
    ext_pos = start - reach + jnp.arange(rows + 2 * reach, dtype=jnp.int32)
    own_q = queries[0]
    own_k = keys[0]
    own_v = values[0]
    own_grad = grad_out[0]
    rims = padded(jnp.stack([own_k, own_v]), (("tm", 1),), reach)
    ext_keys = rims[0]
    ext_values = rims[1]
    weight = lax.all_gather(out_weight, "dp", axis=0, tiled=True)
    allowed = window_mask(query_pos, ext_pos, length, reach)
    scores = (
        jnp.einsum(
            "rhd,shd->hrs",
            split_heads(own_q, H),
            split_heads(ext_keys, H),
            preferred_element_type=jnp.float32,
        )
        * scale
    )
    log_total, probs_f = normalize(scores, allowed)
    probs = probs_f.astype(jnp.bfloat16)
    attn_out = (
        jnp.einsum(
            "hrs,shd->rhd", probs, split_heads(ext_values, H), preferred_element_type=jnp.float32
        )
        .reshape(rows, width)
        .astype(jnp.bfloat16)
    )
    valid = (query_pos < length)[:, None]
    attended = jnp.where(valid, jnp.dot(attn_out, weight, preferred_element_type=jnp.float32), 0.0)
    attended = attended.astype(jnp.bfloat16)
    masked_grad = jnp.where(valid, own_grad, jnp.zeros_like(own_grad))
    grad_attn = lax.dot_general(
        masked_grad, weight, (((1,), (1,)), ((), ())), preferred_element_type=jnp.float32
    ).astype(jnp.bfloat16)
    grad_probs = jnp.einsum(
        "rhd,shd->hrs",
        split_heads(grad_attn, H),
        split_heads(ext_values, H),
        preferred_element_type=jnp.float32,
    )
    row_delta = jnp.sum(probs_f * grad_probs, axis=-1)
    grad_scores = (probs_f * (grad_probs - row_delta[..., None]) * scale).astype(jnp.bfloat16)
    grad_queries = (
        jnp.einsum(
            "hrs,shd->rhd",
            grad_scores,
            split_heads(ext_keys, H),
            preferred_element_type=jnp.float32,
        )
        .reshape(rows, width)
        .astype(jnp.bfloat16)
    )
    key_terms = jnp.einsum(
        "hrs,rhd->shd", grad_scores, split_heads(own_q, H), preferred_element_type=jnp.float32
    ).reshape(rows + 2 * reach, width)
    value_terms = jnp.einsum(
        "hrs,rhd->shd", probs, split_heads(grad_attn, H), preferred_element_type=jnp.float32
    ).reshape(rows + 2 * reach, width)
    both_terms = jnp.stack([key_terms, value_terms])
    outer = jnp.concatenate([both_terms[:, :reach], both_terms[:, rows + reach :]], axis=1)
    returned = padded(outer, (("tm", 1),), reach)
    summed = both_terms[:, reach : reach + rows]
    summed = summed + jnp.pad(returned[:, :reach], ((0, 0), (0, rows - reach), (0, 0)))
    summed = summed + jnp.pad(returned[:, 3 * reach :], ((0, 0), (rows - reach, 0), (0, 0)))
    grad_keys = summed[0].astype(jnp.bfloat16)
    grad_values = summed[1].astype(jnp.bfloat16)
    piece = width // (tm_size * dp_size)
    reordered = (
        attn_out.reshape(rows, dp_size, tm_size, piece).transpose(0, 2, 1, 3).reshape(rows, width)
    )
    shard = lax.psum_scatter(
        lax.dot_general(
            reordered, masked_grad, (((0,), (0,)), ((), ())), preferred_element_type=jnp.float32
        )
        * inv_count,
        ("tm", "dp"),
        scatter_dimension=0,
        tiled=True,
    )
    grad_weight = lax.all_gather(shard, "tm", axis=0, tiled=True)
    return (attended[None], grad_queries[None], grad_keys[None], grad_values[None], grad_weight)


def solution(mesh):
    placed = (
        P(("groups", "dp"), "tm", None),
        P(("groups", "dp"), "tm", None),
        P(("groups", "dp"), "tm", None),
        P(("groups", "dp")),
        P("dp", None),
        P(("groups", "dp"), "tm", None),
    )
    return jax.shard_map(
        per_device,
        mesh=mesh,
        in_specs=placed,
        out_specs=(
            P(("groups", "dp"), "tm", None),
            P(("groups", "dp"), "tm", None),
            P(("groups", "dp"), "tm", None),
            P(("groups", "dp"), "tm", None),
            P(("groups", "dp"), None),
        ),
        check_vma=False,
    )
```

profile of v0, /device:TPU:1, one launch (start us, length us, event | category | flops | bytes accessed | tf_op | source)
XLA Modules:
  0.0 222.7 jit_solution(43851631501471699)
XLA Ops:
  8.0 0.0 all-gather.3.cloned.1.call-start
  8.1 0.7 all-gather.3.cloned.1.call-update
  8.7 0.0 reduce-scatter.2.cloned.1.call-start
  8.8 1.2 copy.27
  10.0 1.2 copy.28
  11.3 0.2 fusion.28
  11.5 2.0 collective-permute-start.1
  13.5 4.6 %collective-permute-start = (bf16[2,128,1024]{1,2,0:T(8,128)(2,1)S(1)}, bf16[2,128,1024]{1,2,0:T(8,128)(2,1)}, u32[]{:S(2)}, u32[]{:S(2)}) collective-permute-start(bf16[2,128,1024]{1,2,0:T(8,128)(2,1)S(1)} %get-tuple-element.21), channel_id=1, source_target_pairs={{0,4},{4,8},{8,12},{12,16},{16,20},{20,24},{24,28},{1,5},{5,9},{9,... | collective-permute-start | bytes 1572872 | tf_op jit(solution)/shard_map/ppermute | solution.py:20
  18.7 0.2 copy.52
  18.9 0.2 fusion.34
  19.2 3.8 %collective-permute-done.1 = bf16[2,128,1024]{1,2,0:T(8,128)(2,1)} collective-permute-done((bf16[2,128,1024]{1,2,0:T(8,128)(2,1)S(1)}, bf16[2,128,1024]{1,2,0:T(8,128)(2,1)}, u32[]{:S(2)}, u32[]{:S(2)}) %collective-permute-start.1) | collective-permute-done | bytes 524320 | tf_op jit(solution)/shard_map/ppermute | solution.py:23
  23.0 1.1 collective-permute-done
  24.1 1.4 pad_maximum_fusion
  25.5 0.1 fusion.50
  25.7 0.0 copy-start.2
  25.7 1.0 copy-done.2
  26.7 0.9 fusion.4
  27.6 0.9 exponential_reduce_fusion
  28.5 0.0 copy-start.5
  28.5 1.2 convolution_convert_fusion
  29.7 0.0 copy-done
  29.7 0.0 copy-start.4
  29.8 0.2 copy-done.5
  29.9 2.7 %convolution_multiply_fusion = f32[1024,1024]{1,0:T(8,128)} fusion(bf16[256,1024]{0,1:T(8,128)(2,1)S(1)} %bitcast.84, bf16[1,256,1024]{2,1,0:T(8,128)(2,1)S(1)} %copy-done.5, pred[256]{0:T(512)(128)(4,1)S(1)} %get-tuple-element.26), kind=kOutput, calls=%fused_computation.16 | convolution fusion | flops 538181632 | bytes 5243136 | tf_op jit(solution)/shard_map/dot_general | solution.py:131
  32.7 0.0 reduce-scatter.2.cloned.1.call-update
  32.7 0.0 all-gather.5.cloned.1.call-start
  32.7 16.1 %all-gather.3.cloned.1.call-done = bf16[1024,1024]{1,0:T(8,128)(2,1)} async-done(((bf16[256,1024]{1,0:T(8,128)(2,1)}), bf16[1024,1024]{1,0:T(8,128)(2,1)}) %all-gather.3.cloned.1.call-update) | async-done | bytes 2097168 | tf_op jit(solution)/shard_map/all_gather | solution.py:67
  48.8 2.3 %convolution_convert_fusion.1 = bf16[256,1024]{1,0:T(8,128)(2,1)S(1)} fusion(bf16[1024,1024]{1,0:T(8,128)(2,1)} %all-gather.3.cloned.1.call-done, bf16[1,256,1024]{2,1,0:T(8,128)(2,1)S(1)} %copy-done.5, pred[256]{0:T(512)(128)(4,1)S(1)} %get-tuple-element.26), kind=kOutput, calls=%fused_computation.26 | convolution fusion | flops 537395200 | bytes 3145984 | tf_op jit(solution)/shard_map/dot_general | solution.py:91
  51.2 0.2 copy.53
  51.4 2.7 %fusion.52 = f32[8,256,512]{1,2,0:T(8,128)} fusion(bf16[256,8,128]{0,2,1:T(8,128)(2,1)S(1)} %bitcast.78, bf16[512,8,128]{0,2,1:T(8,128)(2,1)S(1)} %bitcast.83), kind=kOutput, calls=%fused_computation.63 | convolution fusion | flops 268435456 | bytes 5767168 | tf_op jit(solution)/shard_map/rhd,shd->hrs/dot_general | solution.py:94
  54.1 9.9 %fusion.8 = f32[8,512,128]{1,2,0:T(8,128)} fusion(bf16[256,8,128]{0,2,1:T(8,128)(2,1)S(1)} %bitcast.86, f32[8,256,512]{1,2,0:T(8,128)} %fusion.52, f32[8,512,256]{2,1,0:T(8,128)} %copy-done, f32[8,256]{1,0:T(8,128)S(1)} %log_add_fusion, pred[256,512]{0,1:T(8,128)(4,1)S(1)} %fusion.34), kind=kOutput, calls=%fused_computation.14 | convolution fusion | flops 279972352 | bytes 11149312 | tf_op jit(solution)/shard_map/hrs,rhd->shd/dot_general | solution.py:112
  64.0 1.9 copy.41
  65.9 109.8 %reduce-scatter.2.cloned.1.call-done = f32[32,1024]{1,0:T(8,128)} async-done(((f32[1024,1024]{1,0:T(8,128)}), f32[32,1024]{1,0:T(8,128)}) %reduce-scatter.2.cloned.1.call-update) | async-done | bytes 131088 | tf_op jit(solution)/shard_map/reduce_scatter | solution.py:130
  175.7 0.0 all-gather.5.cloned.1.call-update
  175.8 4.7 %fusion.25 = f32[8,128,512]{2,1,0:T(8,128)} fusion(bf16[256,8,128]{0,2,1:T(8,128)(2,1)S(1)} %bitcast.79, f32[8,512,256]{2,1,0:T(8,128)} %copy-done, f32[8,256]{1,0:T(8,128)S(1)} %log_add_fusion, pred[256,512]{0,1:T(8,128)(4,1)S(1)} %fusion.34), kind=kOutput, calls=%fused_computation.34 | convolution fusion | flops 272629760 | bytes 6955008 | tf_op jit(solution)/shard_map/hrs,rhd->shd/dot_general | solution.py:115
  180.5 2.9 %copy.42 = f32[1,512,1024]{2,1,0:T(8,128)} copy(f32[1,512,1024]{1,2,0:T(8,128)} %bitcast.77) | data formatting | bytes 4194304 | tf_op jit(solution)/shard_map/stack;reshape | solution.py:118
  183.4 2.8 %fusion.24 = (f32[2,128,1024]{2,1,0:T(8,128)}, f32[2,128,1024]{2,1,0:T(8,128)}) fusion(f32[1,512,1024]{2,1,0:T(8,128)S(1)} %copy.41, f32[1,512,1024]{2,1,0:T(8,128)} %copy.42), kind=kLoop, calls=%fused_computation.30 | loop fusion | flops 524288 | bytes 6291456 | tf_op jit(solution)/shard_map/stack | solution.py:118
  186.2 6.1 %collective-permute-start.3 = (f32[2,128,1024]{2,1,0:T(8,128)}, f32[2,128,1024]{2,1,0:T(8,128)}, u32[]{:S(2)}, u32[]{:S(2)}) collective-permute-start(f32[2,128,1024]{2,1,0:T(8,128)} %get-tuple-element.16), channel_id=1, source_target_pairs={{4,0},{8,4},{12,8},{16,12},{20,16},{24,20},{28,24},{5,1},{9,5},{13... | collective-permute-start | bytes 3145736 | tf_op jit(solution)/shard_map/ppermute | solution.py:23
  192.3 2.1 collective-permute-start.2
  194.4 0.0 copy-done.3
  194.5 9.4 %fusion.20 = bf16[8,128,256]{2,1,0:T(8,128)(2,1)} fusion(bf16[512,8,128]{0,2,1:T(8,128)(2,1)S(1)} %bitcast.81, f32[8,256,512]{1,2,0:T(8,128)} %fusion.52, f32[8,512,256]{2,1,0:T(8,128)} %copy-done, f32[8,256]{1,0:T(8,128)S(1)} %log_add_fusion, pred[256,512]{0,1:T(8,128)(4,1)S(1)} %fusion.34), kind=kOutput, calls=%fused_computation.28 | convolution fusion | flops 280234496 | bytes 10100736 | tf_op jit(solution)/shard_map/hrs,shd->rhd/dot_general | solution.py:103
  203.8 2.0 copy.44
  205.9 3.4 %fusion.23 = bf16[1,256,1024]{2,1,0:T(8,128)(2,1)} fusion(bf16[256,1024]{0,1:T(8,128)(2,1)} %bitcast.89, bf16[1024,1024]{1,0:T(8,128)(2,1)} %all-gather.3.cloned.1.call-done, pred[256]{0:T(512)(128)(4,1)S(1)} %get-tuple-element.26), kind=kOutput, calls=%fused_computation.29 | convolution fusion | flops 537395200 | bytes 3145984 | tf_op jit(solution)/shard_map/dot_general | solution.py:88
  209.3 0.7 collective-permute-done.3
  210.0 0.0 collective-permute-done.2
  210.0 1.9 fusion.16
  211.9 1.0 fusion.51
  212.9 2.3 %copy.56 = f32[256,1024]{1,0:T(8,128)} copy(f32[256,1024]{1,0:T(8,128)} %all-gather.5.cloned.1.call-done) | data formatting | bytes 2097152
  (14 shorter events, 0.1 us)
Async XLA Ops:
  8.0 10.7 %copy-start.6 = (bf16[1,256,1024]{2,1,0:T(8,128)(2,1)S(1)}, bf16[1,256,1024]{2,1,0:T(8,128)(2,1)}, u32[]{:S(2)}) copy-start(bf16[1,256,1024]{2,1,0:T(8,128)(2,1)} %param.6) | copy-start | bytes 1572868
  8.0 40.8 %all-gather.3.cloned.1.call-start = ((), (), s32[]{:S(2)}) async-start(), calls=%async_computation.1 | async-start | bytes 2621440 | tf_op jit(solution)/shard_map/all_gather | solution.py:67
  8.7 167.0 %reduce-scatter.2.cloned.1.call-start = ((), (), s32[]{:S(2)}) async-start(), calls=%async_computation.2 | async-start | bytes 4325376 | tf_op jit(solution)/shard_map/reduce_scatter | solution.py:130
  11.5 11.6 %collective-permute-start.1 = (bf16[2,128,1024]{1,2,0:T(8,128)(2,1)S(1)}, bf16[2,128,1024]{1,2,0:T(8,128)(2,1)}, u32[]{:S(2)}, u32[]{:S(2)}) collective-permute-start(bf16[2,128,1024]{1,2,0:T(8,128)(2,1)S(1)} %get-tuple-element.22), channel_id=1, source_target_pairs={{4,0},{8,4},{12,8},{16,12},{20,16},{24,20},{28,24},{5,1},{9,5},{13... | collective-permute-start | bytes 1572872 | tf_op jit(solution)/shard_map/ppermute | solution.py:23
  13.5 10.7 %collective-permute-start = (bf16[2,128,1024]{1,2,0:T(8,128)(2,1)S(1)}, bf16[2,128,1024]{1,2,0:T(8,128)(2,1)}, u32[]{:S(2)}, u32[]{:S(2)}) collective-permute-start(bf16[2,128,1024]{1,2,0:T(8,128)(2,1)S(1)} %get-tuple-element.21), channel_id=1, source_target_pairs={{0,4},{4,8},{8,12},{12,16},{16,20},{20,24},{24,28},{1,5},{5,9},{9,... | collective-permute-start | bytes 1572872 | tf_op jit(solution)/shard_map/ppermute | solution.py:20
  25.7 1.0 copy-start.2
  27.6 2.1 copy-start
  28.5 1.4 copy-start.5
  29.7 3.0 %copy-start.4 = (bf16[8,128,256]{2,1,0:T(8,128)(2,1)}, bf16[8,128,256]{2,1,0:T(8,128)(2,1)S(1)}, u32[]{:S(2)}) copy-start(bf16[8,128,256]{2,1,0:T(8,128)(2,1)S(1)} %convolution_convert_fusion) | copy-start | bytes 1572868
  32.7 180.2 %all-gather.5.cloned.1.call-start = ((), (), s32[]{:S(2)}) async-start(), calls=%async_computation.3 | async-start | bytes 1179648 | tf_op jit(solution)/shard_map/all_gather | solution.py:139
  183.4 11.0 %copy-start.3 = (bf16[1,512,1024]{1,2,0:T(8,128)(2,1)S(1)}, bf16[1,512,1024]{1,2,0:T(8,128)(2,1)}, u32[]{:S(2)}) copy-start(bf16[1,512,1024]{1,2,0:T(8,128)(2,1)} %copy-done.2) | copy-start | bytes 3145732
  186.2 23.8 %collective-permute-start.3 = (f32[2,128,1024]{2,1,0:T(8,128)}, f32[2,128,1024]{2,1,0:T(8,128)}, u32[]{:S(2)}, u32[]{:S(2)}) collective-permute-start(f32[2,128,1024]{2,1,0:T(8,128)} %get-tuple-element.16), channel_id=1, source_target_pairs={{4,0},{8,4},{12,8},{16,12},{20,16},{24,20},{28,24},{5,1},{9,5},{13... | collective-permute-start | bytes 3145736 | tf_op jit(solution)/shard_map/ppermute | solution.py:23
  192.3 17.7 %collective-permute-start.2 = (f32[2,128,1024]{2,1,0:T(8,128)}, f32[2,128,1024]{2,1,0:T(8,128)}, u32[]{:S(2)}, u32[]{:S(2)}) collective-permute-start(f32[2,128,1024]{2,1,0:T(8,128)} %get-tuple-element.15), channel_id=1, source_target_pairs={{0,4},{4,8},{8,12},{12,16},{16,20},{20,24},{24,28},{1,5},{5,9},{9,... | collective-permute-start | bytes 3145736 | tf_op jit(solution)/shard_map/ppermute | solution.py:20
  205.9 4.1 %copy-start.1 = (f32[1,512,1024]{2,1,0:T(8,128)S(1)}, f32[1,512,1024]{2,1,0:T(8,128)}, u32[]{:S(2)}) copy-start(f32[1,512,1024]{2,1,0:T(8,128)} %copy.42) | copy-start | bytes 6291460
Sparse Core Ops, SparseCore 0:
  10.7 38.0 all-gather.2
Sparse Core Ops, SparseCore 1:
  32.8 142.9 reduce-scatter.1
  177.2 28.1 all-gather.4
where the time goes:
time: 224 us; the launch traced here: 223 us
  waiting for transfers between devices  132 us (59%)
  matrix products  37.3 us (17%)
  between operations  16.4 us (7%)
  starting transfers between devices  14.9 us (7%)
  local copies, waits for them, and re-layouts  14.5 us (6%)
  other arithmetic  7.42 us (3%)
    reduce_scatter x1, waiting for transfers between devices, per_device(): lax.psum_scatter(lax.dot_general(reordered, masked_grad, (((0,), (0,)), (...  110 us
    all_gather x1, waiting for transfers between devices, per_device(): weight = lax.all_gather(out_weight, 'dp', axis=0, tiled=True)  16.1 us
    dot_general x1, matrix products, per_device(): jnp.einsum('hrs,rhd->shd', grad_scores, split_heads(own_q, H), preferred_...  9.89 us
    dot_general x1, matrix products, per_device(): jnp.einsum('hrs,shd->rhd', grad_scores, split_heads(ext_keys, H), preferr...  9.39 us
    ppermute x2, starting transfers between devices, padded(): lax.ppermute(lax.slice_in_dim(block, 0, width, axis=dim), axis, backward)  8.09 us
    unnamed x18, local copies, waits for them, and re-layouts  7.98 us
    ppermute x2, starting transfers between devices, padded(): lax.ppermute(lax.slice_in_dim(block, block.shape[dim] - width, None, axis...  6.65 us
    another operation x2, local copies, waits for them, and re-layouts, per_device(): both_terms = jnp.stack([key_terms, value_terms])  4.86 us
  transfers between devices with their start and end apart: 7, of which 5 were waited for; matrix products, arithmetic and copies ran while one was open for 25% of the time, Pallas kernels for 0%

commit v1 on v0

v1 whole, which is shorter than its diff:
```python
import functools
import math

import jax
import jax.numpy as jnp
from jax import lax
from jax.experimental import pallas as pl
from jax.experimental.pallas import tpu as pltpu
from jax.sharding import PartitionSpec as P

H = 8
WIN = 128
CHUNKS = 2
NEG_FILL = -1000000000.0
F32 = jnp.float32
BF16 = jnp.bfloat16


def dot(a, b, over_a, over_b):
    return lax.dot_general(a, b, (((over_a,), (over_b,)), ((), ())), preferred_element_type=F32)


def piece_grid(nz, shard, cols):
    down = min(nz, shard // 16)
    across = nz // down
    return down, across, shard // down, cols // across


def kernel(
    n_tm, n_dp, inv_count,
    len_ref, q_ref, k_hbm, v_hbm, w_hbm, g_ref,
    att_ref, dq_ref, dk_ref, dv_ref, gw_ref,
    kext, vext, wfull, gm, gsplit, gg, ao, ga, probs, mids, halo_out, halo_in,
    part_out, part_in, acc, z_own, z_out, z_in, final,
    own_sem, kv_send, kv_recv, w_send, w_recv, wf_send, wf_recv, g_send, g_recv,
    ao_send, ao_recv, h_send, h_recv, p_send, p_recv, z_send, z_recv,
    f_send, f_recv, x_send, x_recv,
):
    rows, width = q_ref.shape
    shard = width // n_dp
    half = shard // 2
    head = width // H
    heads = shard // head
    nz = n_tm // 2
    cols = width // 2
    ccols = cols // CHUNKS
    scale = 1.0 / math.sqrt(head)
    down, across, prow, pcol = piece_grid(nz, shard, ccols)

    tm = lax.axis_index("tm")
    dp = lax.axis_index("dp")
    z = tm // 2
    core = tm % 2
    partner = tm + 1 - 2 * core
    right = lax.rem(tm + 1, n_tm)
    left = lax.rem(tm + n_tm - 1, n_tm)
    has_left = tm > 0
    has_right = tm < n_tm - 1

    def peer(k):
        return lax.rem(dp + k, n_dp)

    def z_peer(k):
        return lax.rem(z + k, nz)

    def remote(src, dst, send, recv, **where):
        return pltpu.make_async_remote_copy(
            src_ref=src, dst_ref=dst, send_sem=send, recv_sem=recv,
            device_id=where, device_id_type=pl.DeviceIdType.MESH,
        )

    own = [
        pltpu.make_async_copy(k_hbm, kext.at[pl.ds(WIN, rows)], own_sem.at[0]),
        pltpu.make_async_copy(v_hbm, vext.at[pl.ds(WIN, rows)], own_sem.at[1]),
        pltpu.make_async_copy(w_hbm, wfull.at[dp], own_sem.at[2]),
    ]
    for copy in own:
        copy.start()

    barrier = pltpu.get_barrier_semaphore()
    for t in (left, right):
        pl.semaphore_signal(barrier, inc=1, device_id={"tm": t}, device_id_type=pl.DeviceIdType.MESH)
    for k in range(1, n_dp):
        pl.semaphore_signal(barrier, inc=1, device_id={"dp": peer(k)}, device_id_type=pl.DeviceIdType.MESH)
    for k in range(1, nz):
        pl.semaphore_signal(
            barrier, inc=1, device_id={"tm": 2 * z_peer(k) + core}, device_id_type=pl.DeviceIdType.MESH
        )
    pl.semaphore_wait(barrier, 2 + (n_dp - 1) + (nz - 1))

    to_right, to_left = [], []
    for i, (src, ext) in enumerate(((k_hbm, kext), (v_hbm, vext))):
        to_right.append(
            remote(src.at[pl.ds(rows - WIN, WIN)], ext.at[pl.ds(0, WIN)],
                   kv_send.at[0, i], kv_recv.at[0, i], tm=right)
        )
        to_left.append(
            remote(src.at[pl.ds(0, WIN)], ext.at[pl.ds(WIN + rows, WIN)],
                   kv_send.at[1, i], kv_recv.at[1, i], tm=left)
        )

    @pl.when(has_right)
    def _():
        for copy in to_right:
            copy.start()

    @pl.when(has_left)
    def _():
        for copy in to_left:
            copy.start()

    w_half = pl.ds(pl.multiple_of(core * half, half), half)
    w_copies = [
        remote(w_hbm.at[w_half], wfull.at[dp, w_half], w_send.at[k], w_recv.at[k], dp=peer(k + 1))
        for k in range(n_dp - 1)
    ]
    for copy in w_copies:
        copy.start()

    length = len_ref[0]
    start = tm * rows
    row_pos = start + lax.broadcasted_iota(jnp.int32, (rows, 1), 0)
    valid = row_pos < length
    masked_grad = jnp.where(valid, g_ref[...].astype(F32), 0.0).astype(BF16)
    gm[...] = masked_grad
    gsplit[0] = masked_grad[:, :cols]
    gsplit[1] = masked_grad[:, cols:]
    g_copy = remote(gsplit.at[1 - core], gg.at[pl.ds(rows, rows)], g_send, g_recv, tm=partner)
    g_copy.start()
    gg[pl.ds(0, rows), :] = gsplit[core]

    @pl.when(jnp.logical_not(has_left))
    def _():
        kext[pl.ds(0, WIN), :] = jnp.zeros((WIN, width), BF16)
        vext[pl.ds(0, WIN), :] = jnp.zeros((WIN, width), BF16)
        halo_in[:, 1] = jnp.zeros((n_dp, 2, WIN, shard), BF16)

    @pl.when(jnp.logical_not(has_right))
    def _():
        kext[pl.ds(WIN + rows, WIN), :] = jnp.zeros((WIN, width), BF16)
        vext[pl.ds(WIN + rows, WIN), :] = jnp.zeros((WIN, width), BF16)
        halo_in[:, 0] = jnp.zeros((n_dp, 2, WIN, shard), BF16)

    for copy in own:
        copy.wait()

    @pl.when(has_left)
    def _():
        for copy in to_right:
            copy.wait_recv()

    @pl.when(has_right)
    def _():
        for copy in to_left:
            copy.wait_recv()

    span = rows + 2 * WIN
    q_pos = start + lax.broadcasted_iota(jnp.int32, (rows, span), 0)
    k_pos = start - WIN + lax.broadcasted_iota(jnp.int32, (rows, span), 1)
    allowed = (jnp.abs(q_pos - k_pos) <= WIN) & (k_pos >= 0) & (k_pos < length)
    bias = jnp.where(allowed, 0.0, NEG_FILL)
    live = jnp.where(valid, 1.0, 0.0)

    def ao_copy(s):
        return remote(
            ao.at[s, pl.ds(0, rows)], ao.at[s, pl.ds(rows, rows)], ao_send.at[s], ao_recv.at[s], tm=partner
        )

    @pl.loop(0, n_dp)
    def _(s):
        at = pl.ds(pl.multiple_of(s * shard, shard), shard)
        q, k, v = q_ref[:, at], kext[:, at], vext[:, at]
        for i in range(heads):
            lanes = slice(i * head, (i + 1) * head)
            masked = dot(q[:, lanes], k[:, lanes], 1, 1) * scale + bias
            top = jnp.max(masked, axis=-1, keepdims=True)
            e = jnp.exp(masked - top)
            p = e * (live / jnp.sum(e, axis=-1, keepdims=True))
            probs[s * heads + i] = p
            ao[s, pl.ds(0, rows), lanes] = dot(p.astype(BF16), v[:, lanes], 1, 0).astype(BF16)
        ao_copy(s).start()

    def w_forward(k):
        src = lax.rem(dp + n_dp - 1 - k, n_dp)
        return remote(
            wfull.at[src, w_half], wfull.at[src, w_half], wf_send.at[k], wf_recv.at[k], tm=partner
        )

    for k in range(n_dp - 1):
        w_copies[k].wait_recv()
        w_forward(k).start()

    g_copy.wait_recv()
    for s in range(n_dp):
        ao_copy(s).wait_recv()

    def part_copy(c, k):
        return remote(
            part_out.at[c, k], part_in.at[c, k], p_send.at[c, k], p_recv.at[c, k], dp=peer(k + 1)
        )

    for c in range(CHUNKS):
        g_cols = gg[:, c * ccols:(c + 1) * ccols]
        for k in range(n_dp - 1):
            part_out[c, k] = dot(ao[peer(k + 1)], g_cols, 0, 0).astype(BF16)
            part_copy(c, k).start()
    for c in range(CHUNKS):
        acc[c] = dot(ao[dp], gg[:, c * ccols:(c + 1) * ccols], 0, 0)

    for k in range(n_dp - 1):
        w_forward(k).wait_recv()

    def halo_copy(s, side):
        return remote(
            halo_out.at[s, side], halo_in.at[s, side], h_send.at[s, side], h_recv.at[s, side],
            tm=(left, right)[side],
        )

    @pl.loop(0, n_dp)
    def _(s):
        at = pl.ds(pl.multiple_of(s * shard, shard), shard)
        q, k, v = q_ref[:, at], kext[:, at], vext[:, at]
        grad_attn = dot(gm[...], wfull[s], 1, 1).astype(BF16)
        for i in range(heads):
            lanes = slice(i * head, (i + 1) * head)
            p = probs[s * heads + i]
            grad_probs = dot(grad_attn[:, lanes], v[:, lanes], 1, 1)
            delta = jnp.sum(p * grad_probs, axis=-1, keepdims=True)
            grad_scores = (p * (grad_probs - delta) * scale).astype(BF16)
            hd = pl.ds(pl.multiple_of(s * shard + i * head, head), head)
            dq_ref[:, hd] = dot(grad_scores, k[:, lanes], 1, 0).astype(BF16)
            terms = (
                dot(grad_scores, q[:, lanes], 0, 0),
                dot(p.astype(BF16), grad_attn[:, lanes], 0, 0),
            )
            for which, term in enumerate(terms):
                halo_out[s, 0, which, :, lanes] = term[:WIN].astype(BF16)
                halo_out[s, 1, which, :, lanes] = term[WIN + rows:].astype(BF16)
                mids[which, :, hd] = term[WIN:WIN + rows]

        @pl.when(has_left)
        def _():
            halo_copy(s, 0).start()

        @pl.when(has_right)
        def _():
            halo_copy(s, 1).start()

    def z_copy(c, k):
        return remote(
            z_out.at[c, z_peer(k + 1)], z_in.at[c, k], z_send.at[c, k], z_recv.at[c, k],
            tm=2 * z_peer(k + 1) + core,
        )

    def final_copy(c, k):
        return remote(
            final.at[core, c, z], final.at[core, c, z], f_send.at[c, k], f_recv.at[c, k],
            tm=2 * z_peer(k + 1) + core,
        )

    def cross_copy(c):
        return remote(final.at[core, c], final.at[core, c], x_send.at[c], x_recv.at[c], tm=partner)

    def cut(j):
        r, a = (j // across) * prow, (j % across) * pcol
        return slice(r, r + prow), slice(a, a + pcol)

    def scatter(c):
        total = acc[c]
        for k in range(n_dp - 1):
            part_copy(c, k).wait_recv()
            total = total + part_in[c, k].astype(F32)
        for j in range(nz):
            r, a = cut(j)
            z_own[c, j] = total[r, a]
            z_out[c, j] = total[r, a].astype(BF16)
        for k in range(nz - 1):
            z_copy(c, k).start()

    def gather(c):
        total = z_own[c, z]
        for k in range(nz - 1):
            z_copy(c, k).wait_recv()
            total = total + z_in[c, k].astype(F32)
        final[core, c, z] = (total * inv_count).astype(BF16)
        for k in range(nz - 1):
            final_copy(c, k).start()

    def cross(c):
        for k in range(nz - 1):
            final_copy(c, k).wait_recv()
        cross_copy(c).start()

    for c in range(CHUNKS):
        scatter(c)

    attended = dot(ao[0, pl.ds(0, rows)], wfull[0], 1, 0)
    for s in range(1, n_dp):
        attended += dot(ao[s, pl.ds(0, rows)], wfull[s], 1, 0)
    att_ref[...] = jnp.where(valid, attended, 0.0).astype(BF16)

    for c in range(CHUNKS):
        gather(c)

    @pl.when(has_right)
    def _():
        for s in range(n_dp):
            halo_copy(s, 0).wait_recv()

    @pl.when(has_left)
    def _():
        for s in range(n_dp):
            halo_copy(s, 1).wait_recv()

    for which, out in enumerate((dk_ref, dv_ref)):
        for s in range(n_dp):
            lanes = slice(s * shard, (s + 1) * shard)
            out[0:WIN, lanes] = (
                mids[which, 0:WIN, lanes] + halo_in[s, 1, which].astype(F32)
            ).astype(BF16)
            if rows > 2 * WIN:
                out[WIN:rows - WIN, lanes] = mids[which, WIN:rows - WIN, lanes].astype(BF16)
            out[rows - WIN:rows, lanes] = (
                mids[which, rows - WIN:rows, lanes] + halo_in[s, 0, which].astype(F32)
            ).astype(BF16)

    for c in range(CHUNKS):
        cross(c)
    for c in range(CHUNKS):
        cross_copy(c).wait_recv()
    for side in range(2):
        for c in range(CHUNKS):
            for j in range(nz):
                r, a = cut(j)
                base = side * cols + c * ccols
                gw_ref[r, base + a.start:base + a.stop] = final[side, c, j].astype(F32)

    @pl.when(has_right)
    def _():
        for copy in to_right:
            copy.wait_send()
        for s in range(n_dp):
            halo_copy(s, 1).wait_send()

    @pl.when(has_left)
    def _():
        for copy in to_left:
            copy.wait_send()
        for s in range(n_dp):
            halo_copy(s, 0).wait_send()

    g_copy.wait_send()
    for k in range(n_dp - 1):
        w_copies[k].wait_send()
        w_forward(k).wait_send()
    for s in range(n_dp):
        ao_copy(s).wait_send()
    for c in range(CHUNKS):
        for k in range(n_dp - 1):
            part_copy(c, k).wait_send()
        for k in range(nz - 1):
            z_copy(c, k).wait_send()
            final_copy(c, k).wait_send()
        cross_copy(c).wait_send()


def per_device(queries, keys, values, lengths, out_weight, grad_out):
    n_tm = lax.axis_size("tm")
    n_dp = lax.axis_size("dp")
    rows, width = queries.shape[1:]
    shard = width // n_dp
    span = rows + 2 * WIN
    nz = n_tm // 2
    cols = width // 2
    ccols = cols // CHUNKS
    _, _, prow, pcol = piece_grid(nz, shard, ccols)
    inv_count = 1.0 / math.sqrt(n_dp * rows * n_tm)
    vmem = pl.BlockSpec(memory_space=pltpu.VMEM)
    hbm = pl.BlockSpec(memory_space=pl.ANY)
    dma = pltpu.SemaphoreType.DMA
    block = jax.ShapeDtypeStruct((rows, width), BF16)
    outs = pl.pallas_call(
        functools.partial(kernel, n_tm, n_dp, inv_count),
        out_shape=(block, block, block, block, jax.ShapeDtypeStruct((shard, width), F32)),
        in_specs=[pl.BlockSpec(memory_space=pltpu.SMEM), vmem, hbm, hbm, hbm, vmem],
        out_specs=(vmem,) * 5,
        scratch_shapes=[
            pltpu.VMEM((span, width), BF16),
            pltpu.VMEM((span, width), BF16),
            pltpu.VMEM((n_dp, shard, width), BF16),
            pltpu.VMEM((rows, width), BF16),
            pltpu.VMEM((2, rows, cols), BF16),
            pltpu.VMEM((2 * rows, cols), BF16),
            pltpu.VMEM((n_dp, 2 * rows, shard), BF16),
            pltpu.VMEM((rows, shard), BF16),
            pltpu.VMEM((H, rows, span), F32),
            pltpu.VMEM((2, rows, width), F32),
            pltpu.VMEM((n_dp, 2, 2, WIN, shard), BF16),
            pltpu.VMEM((n_dp, 2, 2, WIN, shard), BF16),
            pltpu.VMEM((CHUNKS, n_dp - 1, shard, ccols), BF16),
            pltpu.VMEM((CHUNKS, n_dp - 1, shard, ccols), BF16),
            pltpu.VMEM((CHUNKS, shard, ccols), F32),
            pltpu.VMEM((CHUNKS, nz, prow, pcol), F32),
            pltpu.VMEM((CHUNKS, nz, prow, pcol), BF16),
            pltpu.VMEM((CHUNKS, nz - 1, prow, pcol), BF16),
            pltpu.VMEM((2, CHUNKS, nz, prow, pcol), BF16),
            dma((3,)),
            dma((2, 2)), dma((2, 2)),
            dma((n_dp - 1,)), dma((n_dp - 1,)),
            dma((n_dp - 1,)), dma((n_dp - 1,)),
            dma(()), dma(()),
            dma((n_dp,)), dma((n_dp,)),
            dma((n_dp, 2)), dma((n_dp, 2)),
            dma((CHUNKS, n_dp - 1)), dma((CHUNKS, n_dp - 1)),
            dma((CHUNKS, nz - 1)), dma((CHUNKS, nz - 1)),
            dma((CHUNKS, nz - 1)), dma((CHUNKS, nz - 1)),
            dma((CHUNKS,)), dma((CHUNKS,)),
        ],
        compiler_params=pltpu.CompilerParams(
            collective_id=0, has_side_effects=True, vmem_limit_bytes=48 * 1024 * 1024
        ),
        cost_estimate=pl.CostEstimate(flops=4_000_000_000, bytes_accessed=8_000_000, transcendentals=1_000_000),
    )(lengths, queries[0], keys[0], values[0], out_weight, grad_out[0])
    attended, dq, dk, dv, gw = outs
    return (attended[None], dq[None], dk[None], dv[None], gw)


def solution(mesh):
    frames = P(("groups", "dp"), "tm", None)
    return jax.shard_map(
        per_device,
        mesh=mesh,
        in_specs=(frames, frames, frames, P(("groups", "dp")), P("dp", None), frames),
        out_specs=(frames, frames, frames, frames, P(("groups", "dp"), None)),
        check_vma=False,
    )
```

time: 224 us -> 55.9 us (0.25)
  waiting for transfers between devices: 132 us -> 0 us
  Pallas kernels: 0 us -> 44.9 us
  matrix products: 37.3 us -> 0 us
  between operations: 16.4 us -> 1.3 us
  starting transfers between devices: 14.9 us -> 0 us
  other arithmetic: 7.42 us -> 0 us
  local copies, waits for them, and re-layouts: 14.5 us -> 9.34 us
    reduce_scatter x1 -> x0, waiting for transfers between devices: 110 us -> none  [per_device(): lax.psum_scatter(lax.dot_general(reordered, masked_grad, (((0,), (0,)), (...]
    pallas_call x0 -> x1, Pallas kernels: none -> 44.9 us  [per_device(): pl.pallas_call(functools.partial(kernel, n_tm, n_dp, inv_count), out_shap...]
    dot_general x9 -> x0, matrix products: 37.3 us -> none  [the longest x1 9.89 us: per_device(): jnp.einsum('hrs,rhd->shd', grad_scores, split_heads(own_q, H), preferred_...]
    all_gather x2 -> x0, waiting for transfers between devices: 16.1 us -> none  [the longest x1 16.1 us: per_device(): weight = lax.all_gather(out_weight, 'dp', axis=0, tiled=True)]
    ppermute x4 -> x0, starting transfers between devices: 14.7 us -> none  [the longest x2 8.09 us: padded(): lax.ppermute(lax.slice_in_dim(block, 0, width, axis=dim), axis, backward)]
    ppermute x4 -> x0, waiting for transfers between devices: 5.6 us -> none  [the longest x2 4.52 us: padded(): lax.ppermute(lax.slice_in_dim(block, 0, width, axis=dim), axis, backward)]
    another operation x3 -> x0, local copies, waits for them, and re-layouts: 5.06 us -> none  [the longest x2 4.86 us: per_device(): both_terms = jnp.stack([key_terms, value_terms])]
    another operation x3 -> x0, other arithmetic: 4.84 us -> none  [the longest x1 2.78 us: per_device(): both_terms = jnp.stack([key_terms, value_terms])]
  transfers between devices with their start and end apart: 7 -> 0, of which waited for: 5 -> 0; matrix products, arithmetic and copies ran while one was open for 25% -> 0% of each run, Pallas kernels for 0% -> 0%
where the time goes in v1:
time: 55.9 us; the launch traced here: 55.6 us
  Pallas kernels  44.9 us (80%)
  local copies, waits for them, and re-layouts  9.34 us (17%)
  between operations  1.3 us (2%)
    pallas_call x1, Pallas kernels, per_device(): pl.pallas_call(functools.partial(kernel, n_tm, n_dp, inv_count), out_shap...  44.9 us
    unnamed x15, local copies, waits for them, and re-layouts  9.34 us

profile of v1, /device:TPU:1, one launch (start us, length us, event | category | flops | bytes accessed | tf_op | source)
XLA Modules:
  0.0 55.6 jit_solution(1218424510426327505)
XLA Ops:
  1.3 0.0 copy-start
  1.3 1.0 %copy-done = bf16[1,256,1024]{2,1,0:T(8,128)(2,1)S(1)} copy-done((bf16[1,256,1024]{2,1,0:T(8,128)(2,1)S(1)}, bf16[1,256,1024]{2,1,0:T(8,128)(2,1)}, u32[]{:S(2)}) %copy-start) | copy-done | bytes 524312
  2.3 0.0 copy-start.1
  2.3 1.0 %copy-done.1 = bf16[1,256,1024]{2,1,0:T(8,128)(2,1)S(1)} copy-done((bf16[1,256,1024]{2,1,0:T(8,128)(2,1)S(1)}, bf16[1,256,1024]{2,1,0:T(8,128)(2,1)}, u32[]{:S(2)}) %copy-start.1) | copy-done | bytes 524312
  3.4 0.0 copy-start.2
  3.4 1.0 %copy-done.2 = bf16[1,256,1024]{2,1,0:T(8,128)(2,1)S(1)} copy-done((bf16[1,256,1024]{2,1,0:T(8,128)(2,1)S(1)}, bf16[1,256,1024]{2,1,0:T(8,128)(2,1)}, u32[]{:S(2)}) %copy-start.2) | copy-done | bytes 524312
  4.4 0.0 copy-start.3
  4.4 1.0 %copy-done.3 = bf16[256,1024]{1,0:T(8,128)(2,1)S(1)} copy-done((bf16[256,1024]{1,0:T(8,128)(2,1)S(1)}, bf16[256,1024]{1,0:T(8,128)(2,1)}, u32[]{:S(2)}) %copy-start.3) | copy-done | bytes 524312
  5.4 0.0 copy-start.4
  5.4 1.0 %copy-done.4 = bf16[1,256,1024]{2,1,0:T(8,128)(2,1)S(1)} copy-done((bf16[1,256,1024]{2,1,0:T(8,128)(2,1)S(1)}, bf16[1,256,1024]{2,1,0:T(8,128)(2,1)}, u32[]{:S(2)}) %copy-start.4) | copy-done | bytes 524312
  6.5 44.9 %shard_map.101 = (bf16[256,1024]{1,0:T(8,128)(2,1)S(1)}, bf16[256,1024]{1,0:T(8,128)(2,1)S(1)}, bf16[256,1024]{1,0:T(8,128)(2,1)S(1)}, bf16[256,1024]{1,0:T(8,128)(2,1)S(1)}, f32[256,1024]{1,0:T(8,128)S(1)}) custom-call(s32[1]{0:T(128)S(6)} %copy.16.len_ref, bf16[256,1024]{1,0:T(8,128)(2,1)S(1)} %bitcast.12, bf16[256,1024]{1,0:T(8,128)(2,1)S(1)} %bitcast.13, ...), custom_call_target="tpu_custom_call" | custom-call | flops 4000000000 | bytes 8000000 | tf_op jit(solution)/shard_map/pallas_call | solution.py:382
  51.4 0.8 %copy.17 = bf16[1,256,1024]{2,1,0:T(8,128)(2,1)} copy(bf16[1,256,1024]{2,1,0:T(8,128)(2,1)S(1)} %bitcast.11) | data formatting | bytes 1048576
  52.2 0.8 %copy.18 = bf16[1,256,1024]{2,1,0:T(8,128)(2,1)} copy(bf16[1,256,1024]{2,1,0:T(8,128)(2,1)S(1)} %bitcast.10) | data formatting | bytes 1048576
  53.0 0.8 %copy.19 = bf16[1,256,1024]{2,1,0:T(8,128)(2,1)} copy(bf16[1,256,1024]{2,1,0:T(8,128)(2,1)S(1)} %bitcast.9) | data formatting | bytes 1048576
  53.8 0.8 %copy.20 = bf16[1,256,1024]{2,1,0:T(8,128)(2,1)} copy(bf16[1,256,1024]{2,1,0:T(8,128)(2,1)S(1)} %bitcast.8) | data formatting | bytes 1048576
  54.6 1.0 %copy.21 = f32[256,1024]{1,0:T(8,128)} copy(f32[256,1024]{1,0:T(8,128)S(1)} %get-tuple-element.24) | data formatting | bytes 2097152
Async XLA Ops:
  1.3 1.0 %copy-start = (bf16[1,256,1024]{2,1,0:T(8,128)(2,1)S(1)}, bf16[1,256,1024]{2,1,0:T(8,128)(2,1)}, u32[]{:S(2)}) copy-start(bf16[1,256,1024]{2,1,0:T(8,128)(2,1)} %param.6) | copy-start | bytes 1572868
  2.3 1.0 %copy-start.1 = (bf16[1,256,1024]{2,1,0:T(8,128)(2,1)S(1)}, bf16[1,256,1024]{2,1,0:T(8,128)(2,1)}, u32[]{:S(2)}) copy-start(bf16[1,256,1024]{2,1,0:T(8,128)(2,1)} %param.7) | copy-start | bytes 1572868
  3.4 1.0 %copy-start.2 = (bf16[1,256,1024]{2,1,0:T(8,128)(2,1)S(1)}, bf16[1,256,1024]{2,1,0:T(8,128)(2,1)}, u32[]{:S(2)}) copy-start(bf16[1,256,1024]{2,1,0:T(8,128)(2,1)} %param.8) | copy-start | bytes 1572868
  4.4 1.0 %copy-start.3 = (bf16[256,1024]{1,0:T(8,128)(2,1)S(1)}, bf16[256,1024]{1,0:T(8,128)(2,1)}, u32[]{:S(2)}) copy-start(bf16[256,1024]{1,0:T(8,128)(2,1)} %w_hbm.1) | copy-start | bytes 1572868
  5.4 1.0 %copy-start.4 = (bf16[1,256,1024]{2,1,0:T(8,128)(2,1)S(1)}, bf16[1,256,1024]{2,1,0:T(8,128)(2,1)}, u32[]{:S(2)}) copy-start(bf16[1,256,1024]{2,1,0:T(8,128)(2,1)} %param.11) | copy-start | bytes 1572868

commit v2 on v1

--- a/solution.py
+++ b/solution.py
@@ -11,6 +11,7 @@
 H = 8
 WIN = 128
 CHUNKS = 2
+PARTS = 4
 NEG_FILL = -1000000000.0
 F32 = jnp.float32
 BF16 = jnp.bfloat16
@@ -28,15 +29,15 @@
 
 def kernel(
     n_tm, n_dp, inv_count,
-    len_ref, q_ref, k_hbm, v_hbm, w_hbm, g_ref,
+    len_ref, q_hbm, k_hbm, v_hbm, w_hbm, g_hbm,
     att_ref, dq_ref, dk_ref, dv_ref, gw_ref,
-    kext, vext, wfull, gm, gsplit, gg, ao, ga, probs, mids, halo_out, halo_in,
+    q_ref, g_ref, kext, vext, wfull, gm, gsplit, gg, ao, probs, mids, halo_out, halo_in,
     part_out, part_in, acc, z_own, z_out, z_in, final,
     own_sem, kv_send, kv_recv, w_send, w_recv, wf_send, wf_recv, g_send, g_recv,
     ao_send, ao_recv, h_send, h_recv, p_send, p_recv, z_send, z_recv,
     f_send, f_recv, x_send, x_recv,
 ):
-    rows, width = q_ref.shape
+    rows, width = q_hbm.shape
     shard = width // n_dp
     half = shard // 2
     head = width // H
@@ -73,6 +74,8 @@
         pltpu.make_async_copy(k_hbm, kext.at[pl.ds(WIN, rows)], own_sem.at[0]),
         pltpu.make_async_copy(v_hbm, vext.at[pl.ds(WIN, rows)], own_sem.at[1]),
         pltpu.make_async_copy(w_hbm, wfull.at[dp], own_sem.at[2]),
+        pltpu.make_async_copy(q_hbm, q_ref, own_sem.at[3]),
+        pltpu.make_async_copy(g_hbm, g_ref, own_sem.at[4]),
     ]
     for copy in own:
         copy.start()
@@ -88,26 +91,30 @@
         )
     pl.semaphore_wait(barrier, 2 + (n_dp - 1) + (nz - 1))
 
-    to_right, to_left = [], []
-    for i, (src, ext) in enumerate(((k_hbm, kext), (v_hbm, vext))):
-        to_right.append(
-            remote(src.at[pl.ds(rows - WIN, WIN)], ext.at[pl.ds(0, WIN)],
-                   kv_send.at[0, i], kv_recv.at[0, i], tm=right)
-        )
-        to_left.append(
-            remote(src.at[pl.ds(0, WIN)], ext.at[pl.ds(WIN + rows, WIN)],
-                   kv_send.at[1, i], kv_recv.at[1, i], tm=left)
-        )
-
-    @pl.when(has_right)
-    def _():
-        for copy in to_right:
-            copy.start()
-
-    @pl.when(has_left)
-    def _():
-        for copy in to_left:
-            copy.start()
+    def turn(i):
+        return lax.rem(dp + 1 + i, n_dp)
+
+    def kv_copies(s, side):
+        at = pl.ds(pl.multiple_of(s * shard, shard), shard)
+        src, dst = ((rows - WIN, 0), (0, WIN + rows))[side]
+        return [
+            remote(
+                hbm.at[pl.ds(src, WIN), at], ext.at[pl.ds(dst, WIN), at],
+                kv_send.at[side, which, s], kv_recv.at[side, which, s], tm=(right, left)[side],
+            )
+            for which, (hbm, ext) in enumerate(((k_hbm, kext), (v_hbm, vext)))
+        ]
+
+    for i in range(n_dp):
+        @pl.when(has_right)
+        def _():
+            for copy in kv_copies(turn(i), 0):
+                copy.start()
+
+        @pl.when(has_left)
+        def _():
+            for copy in kv_copies(turn(i), 1):
+                copy.start()
 
     w_half = pl.ds(pl.multiple_of(core * half, half), half)
     w_copies = [
@@ -117,6 +124,7 @@
     for copy in w_copies:
         copy.start()
 
+    own[4].wait()
     length = len_ref[0]
     start = tm * rows
     row_pos = start + lax.broadcasted_iota(jnp.int32, (rows, 1), 0)
@@ -141,18 +149,8 @@
         vext[pl.ds(WIN + rows, WIN), :] = jnp.zeros((WIN, width), BF16)
         halo_in[:, 0] = jnp.zeros((n_dp, 2, WIN, shard), BF16)
 
-    for copy in own:
+    for copy in own[:4]:
         copy.wait()
-
-    @pl.when(has_left)
-    def _():
-        for copy in to_right:
-            copy.wait_recv()
-
-    @pl.when(has_right)
-    def _():
-        for copy in to_left:
-            copy.wait_recv()
 
     span = rows + 2 * WIN
     q_pos = start + lax.broadcasted_iota(jnp.int32, (rows, span), 0)
@@ -166,8 +164,34 @@
             ao.at[s, pl.ds(0, rows)], ao.at[s, pl.ds(rows, rows)], ao_send.at[s], ao_recv.at[s], tm=partner
         )
 
+    def part_copy(c, k):
+        return remote(
+            part_out.at[c, k], part_in.at[c, k], p_send.at[c, k], p_recv.at[c, k], dp=peer(k + 1)
+        )
+
+    def send_part(k):
+        s = peer(k + 1)
+        ao_copy(s).wait_recv()
+        for c in range(CHUNKS):
+            part_out[c, k] = dot(ao[s], gg[:, c * ccols:(c + 1) * ccols], 0, 0).astype(BF16)
+            part_copy(c, k).start()
+
+    g_copy.wait_recv()
+
     @pl.loop(0, n_dp)
-    def _(s):
+    def _(step):
+        s = turn(step)
+
+        @pl.when(has_left)
+        def _():
+            for copy in kv_copies(s, 0):
+                copy.wait_recv()
+
+        @pl.when(has_right)
+        def _():
+            for copy in kv_copies(s, 1):
+                copy.wait_recv()
+
         at = pl.ds(pl.multiple_of(s * shard, shard), shard)
         q, k, v = q_ref[:, at], kext[:, at], vext[:, at]
         for i in range(heads):
@@ -180,36 +204,23 @@
             ao[s, pl.ds(0, rows), lanes] = dot(p.astype(BF16), v[:, lanes], 1, 0).astype(BF16)
         ao_copy(s).start()
 
+        @pl.when(step > 0)
+        def _():
+            send_part(step - 1)
+
+    ao_copy(dp).wait_recv()
+    for c in range(CHUNKS):
+        acc[c] = dot(ao[dp], gg[:, c * ccols:(c + 1) * ccols], 0, 0)
+
+    def w_copy(k):
+        return remote(w_hbm.at[w_half], wfull.at[dp, w_half], w_send.at[k], w_recv.at[k], dp=peer(k + 1))
+
     def w_forward(k):
         src = lax.rem(dp + n_dp - 1 - k, n_dp)
         return remote(
             wfull.at[src, w_half], wfull.at[src, w_half], wf_send.at[k], wf_recv.at[k], tm=partner
         )
 
-    for k in range(n_dp - 1):
-        w_copies[k].wait_recv()
-        w_forward(k).start()
-
-    g_copy.wait_recv()
-    for s in range(n_dp):
-        ao_copy(s).wait_recv()
-
-    def part_copy(c, k):
-        return remote(
-            part_out.at[c, k], part_in.at[c, k], p_send.at[c, k], p_recv.at[c, k], dp=peer(k + 1)
-        )
-
-    for c in range(CHUNKS):
-        g_cols = gg[:, c * ccols:(c + 1) * ccols]
-        for k in range(n_dp - 1):
-            part_out[c, k] = dot(ao[peer(k + 1)], g_cols, 0, 0).astype(BF16)
-            part_copy(c, k).start()
-    for c in range(CHUNKS):
-        acc[c] = dot(ao[dp], gg[:, c * ccols:(c + 1) * ccols], 0, 0)
-
-    for k in range(n_dp - 1):
-        w_forward(k).wait_recv()
-
     def halo_copy(s, side):
         return remote(
             halo_out.at[s, side], halo_in.at[s, side], h_send.at[s, side], h_recv.at[s, side],
@@ -217,7 +228,18 @@
         )
 
     @pl.loop(0, n_dp)
-    def _(s):
+    def _(step):
+        s = lax.rem(dp + n_dp - step, n_dp)
+
+        @pl.when(step < n_dp - 1)
+        def _():
+            w_copy(step).wait_recv()
+            w_forward(step).start()
+
+        @pl.when(step > 0)
+        def _():
+            w_forward(step - 1).wait_recv()
+
         at = pl.ds(pl.multiple_of(s * shard, shard), shard)
         q, k, v = q_ref[:, at], kext[:, at], vext[:, at]
         grad_attn = dot(gm[...], wfull[s], 1, 1).astype(BF16)
@@ -291,14 +313,13 @@
             final_copy(c, k).wait_recv()
         cross_copy(c).start()
 
-    for c in range(CHUNKS):
-        scatter(c)
-
     attended = dot(ao[0, pl.ds(0, rows)], wfull[0], 1, 0)
     for s in range(1, n_dp):
         attended += dot(ao[s, pl.ds(0, rows)], wfull[s], 1, 0)
     att_ref[...] = jnp.where(valid, attended, 0.0).astype(BF16)
 
+    for c in range(CHUNKS):
+        scatter(c)
     for c in range(CHUNKS):
         gather(c)
 
@@ -337,16 +358,16 @@
 
     @pl.when(has_right)
     def _():
-        for copy in to_right:
-            copy.wait_send()
         for s in range(n_dp):
+            for copy in kv_copies(s, 0):
+                copy.wait_send()
             halo_copy(s, 1).wait_send()
 
     @pl.when(has_left)
     def _():
-        for copy in to_left:
-            copy.wait_send()
         for s in range(n_dp):
+            for copy in kv_copies(s, 1):
+                copy.wait_send()
             halo_copy(s, 0).wait_send()
 
     g_copy.wait_send()
@@ -362,6 +383,38 @@
             z_copy(c, k).wait_send()
             final_copy(c, k).wait_send()
         cross_copy(c).wait_send()
+
+
+def hand_over_kernel(count, *refs):
+    srcs, dsts, held = refs[:count], refs[count:2 * count], refs[2 * count:3 * count]
+    sem_in, sem_out = refs[3 * count:]
+    loads, stores = [], []
+    for i in range(count):
+        part = srcs[i].shape[0] // PARTS
+        for j in range(PARTS):
+            at = pl.ds(j * part, part)
+            loads.append(pltpu.make_async_copy(srcs[i].at[at], held[i].at[at], sem_in.at[i, j]))
+            stores.append(pltpu.make_async_copy(held[i].at[at], dsts[i].at[at], sem_out.at[i, j]))
+    for load in loads:
+        load.start()
+    for load, store in zip(loads, stores):
+        load.wait()
+        store.start()
+    for store in stores:
+        store.wait()
+
+
+def hand_over(arrays):
+    hbm = pl.BlockSpec(memory_space=pl.ANY)
+    return pl.pallas_call(
+        functools.partial(hand_over_kernel, len(arrays)),
+        out_shape=tuple(jax.ShapeDtypeStruct(a.shape, a.dtype) for a in arrays),
+        in_specs=[hbm] * len(arrays),
+        out_specs=(hbm,) * len(arrays),
+        scratch_shapes=[pltpu.VMEM(a.shape, a.dtype) for a in arrays]
+        + [pltpu.SemaphoreType.DMA((len(arrays), PARTS))] * 2,
+        compiler_params=pltpu.CompilerParams(vmem_limit_bytes=60 * 1024 * 1024),
+    )(*arrays)
 
 
 def per_device(queries, keys, values, lengths, out_weight, grad_out):
@@ -382,9 +435,11 @@
     outs = pl.pallas_call(
         functools.partial(kernel, n_tm, n_dp, inv_count),
         out_shape=(block, block, block, block, jax.ShapeDtypeStruct((shard, width), F32)),
-        in_specs=[pl.BlockSpec(memory_space=pltpu.SMEM), vmem, hbm, hbm, hbm, vmem],
+        in_specs=[pl.BlockSpec(memory_space=pltpu.SMEM), hbm, hbm, hbm, hbm, hbm],
         out_specs=(vmem,) * 5,
         scratch_shapes=[
+            pltpu.VMEM((rows, width), BF16),
+            pltpu.VMEM((rows, width), BF16),
             pltpu.VMEM((span, width), BF16),
             pltpu.VMEM((span, width), BF16),
             pltpu.VMEM((n_dp, shard, width), BF16),
@@ -392,7 +447,6 @@
             pltpu.VMEM((2, rows, cols), BF16),
             pltpu.VMEM((2 * rows, cols), BF16),
             pltpu.VMEM((n_dp, 2 * rows, shard), BF16),
-            pltpu.VMEM((rows, shard), BF16),
             pltpu.VMEM((H, rows, span), F32),
             pltpu.VMEM((2, rows, width), F32),
             pltpu.VMEM((n_dp, 2, 2, WIN, shard), BF16),
@@ -404,8 +458,8 @@
             pltpu.VMEM((CHUNKS, nz, prow, pcol), BF16),
             pltpu.VMEM((CHUNKS, nz - 1, prow, pcol), BF16),
             pltpu.VMEM((2, CHUNKS, nz, prow, pcol), BF16),
-            dma((3,)),
-            dma((2, 2)), dma((2, 2)),
+            dma((5,)),
+            dma((2, 2, n_dp)), dma((2, 2, n_dp)),
             dma((n_dp - 1,)), dma((n_dp - 1,)),
             dma((n_dp - 1,)), dma((n_dp - 1,)),
             dma(()), dma(()),
@@ -417,11 +471,11 @@
             dma((CHUNKS,)), dma((CHUNKS,)),
         ],
         compiler_params=pltpu.CompilerParams(
-            collective_id=0, has_side_effects=True, vmem_limit_bytes=48 * 1024 * 1024
+            collective_id=0, has_side_effects=True, vmem_limit_bytes=60 * 1024 * 1024
         ),
         cost_estimate=pl.CostEstimate(flops=4_000_000_000, bytes_accessed=8_000_000, transcendentals=1_000_000),
     )(lengths, queries[0], keys[0], values[0], out_weight, grad_out[0])
-    attended, dq, dk, dv, gw = outs
+    attended, dq, dk, dv, gw = hand_over(outs)
     return (attended[None], dq[None], dk[None], dv[None], gw)
 
 

time: 55.9 us -> 48.9 us (0.87)
  local copies, waits for them, and re-layouts: 9.34 us -> 0 us
  Pallas kernels: 44.9 us -> 47.5 us
    unnamed x15 -> x0, local copies, waits for them, and re-layouts: 9.34 us -> none
    pallas_call x0 -> x1, Pallas kernels: none -> 3.26 us  [hand_over(): pl.pallas_call(functools.partial(hand_over_kernel, len(arrays)), out_shap...]
    pallas_call x1, Pallas kernels: 44.9 us -> 44.2 us  [per_device(): pl.pallas_call(functools.partial(kernel, n_tm, n_dp, inv_count), out_shap...]
where the time goes in v2:
time: 48.9 us; the launch traced here: 48.8 us
  Pallas kernels  47.5 us (97%)
  between operations  1.29 us (3%)
    pallas_call x1, Pallas kernels, per_device(): pl.pallas_call(functools.partial(kernel, n_tm, n_dp, inv_count), out_shap...  44.2 us
    pallas_call x1, Pallas kernels, hand_over(): pl.pallas_call(functools.partial(hand_over_kernel, len(arrays)), out_shap...  3.26 us

profile of v2, /device:TPU:1, one launch (start us, length us, event | category | flops | bytes accessed | tf_op | source)
XLA Modules:
  0.0 48.8 jit_solution(8925166508690053380)
XLA Ops:
  1.3 44.2 %shard_map.101 = (bf16[256,1024]{1,0:T(8,128)(2,1)}, bf16[256,1024]{1,0:T(8,128)(2,1)}, bf16[256,1024]{1,0:T(8,128)(2,1)}, bf16[256,1024]{1,0:T(8,128)(2,1)}, f32[256,1024]{1,0:T(8,128)}) custom-call(s32[1]{0:T(128)S(6)} %copy.11.len_ref, bf16[256,1024]{1,0:T(8,128)(2,1)} %bitcast.8, bf16[256,1024]{1,0:T(8,128)(2,1)} %bitcast.9, bf16[256,1024]{1,0:T(8,128)(2,1)} %bitcast.10, ...), custom_call_target="tpu_custom_call" | custom-call | flops 4000000000 | bytes 8000000 | tf_op jit(solution)/shard_map/pallas_call | solution.py:435
  45.5 3.3 %shard_map.102 = (bf16[256,1024]{1,0:T(8,128)(2,1)}, bf16[256,1024]{1,0:T(8,128)(2,1)}, bf16[256,1024]{1,0:T(8,128)(2,1)}, bf16[256,1024]{1,0:T(8,128)(2,1)}, f32[256,1024]{1,0:T(8,128)}) custom-call(bf16[256,1024]{1,0:T(8,128)(2,1)} %get-tuple-element.15.refs_0_, bf16[256,1024]{1,0:T(8,128)(2,1)} %get-tuple-element.16.refs_1_, ...), custom_call_target="tpu_custom_call" | custom-call | tf_op jit(solution)/shard_map/pallas_call | solution.py:409

commit v3 on v2

--- a/solution.py
+++ b/solution.py
@@ -11,7 +11,7 @@
 H = 8
 WIN = 128
 CHUNKS = 2
-PARTS = 4
+PARTS = 2
 NEG_FILL = -1000000000.0
 F32 = jnp.float32
 BF16 = jnp.bfloat16
@@ -313,13 +313,14 @@
             final_copy(c, k).wait_recv()
         cross_copy(c).start()
 
+    for c in range(CHUNKS):
+        scatter(c)
+
     attended = dot(ao[0, pl.ds(0, rows)], wfull[0], 1, 0)
     for s in range(1, n_dp):
         attended += dot(ao[s, pl.ds(0, rows)], wfull[s], 1, 0)
     att_ref[...] = jnp.where(valid, attended, 0.0).astype(BF16)
 
-    for c in range(CHUNKS):
-        scatter(c)
     for c in range(CHUNKS):
         gather(c)
 
@@ -354,7 +355,7 @@
             for j in range(nz):
                 r, a = cut(j)
                 base = side * cols + c * ccols
-                gw_ref[r, base + a.start:base + a.stop] = final[side, c, j].astype(F32)
+                gw_ref[r, base + a.start:base + a.stop] = final[side, c, j]
 
     @pl.when(has_right)
     def _():
@@ -387,18 +388,22 @@
 
 def hand_over_kernel(count, *refs):
     srcs, dsts, held = refs[:count], refs[count:2 * count], refs[2 * count:3 * count]
-    sem_in, sem_out = refs[3 * count:]
+    wide, sem_in, sem_out = refs[3 * count:]
     loads, stores = [], []
     for i in range(count):
         part = srcs[i].shape[0] // PARTS
         for j in range(PARTS):
             at = pl.ds(j * part, part)
             loads.append(pltpu.make_async_copy(srcs[i].at[at], held[i].at[at], sem_in.at[i, j]))
-            stores.append(pltpu.make_async_copy(held[i].at[at], dsts[i].at[at], sem_out.at[i, j]))
+            ready = wide if i == count - 1 else held[i]
+            stores.append(pltpu.make_async_copy(ready.at[at], dsts[i].at[at], sem_out.at[i, j]))
     for load in loads:
         load.start()
-    for load, store in zip(loads, stores):
+    for n, (load, store) in enumerate(zip(loads, stores)):
         load.wait()
+        if n >= (count - 1) * PARTS:
+            at = pl.ds((n - (count - 1) * PARTS) * part, part)
+            wide[at, :] = held[-1][at, :].astype(F32)
         store.start()
     for store in stores:
         store.wait()
@@ -408,10 +413,12 @@
     hbm = pl.BlockSpec(memory_space=pl.ANY)
     return pl.pallas_call(
         functools.partial(hand_over_kernel, len(arrays)),
-        out_shape=tuple(jax.ShapeDtypeStruct(a.shape, a.dtype) for a in arrays),
+        out_shape=tuple(jax.ShapeDtypeStruct(a.shape, a.dtype) for a in arrays[:-1])
+        + (jax.ShapeDtypeStruct(arrays[-1].shape, F32),),
         in_specs=[hbm] * len(arrays),
         out_specs=(hbm,) * len(arrays),
         scratch_shapes=[pltpu.VMEM(a.shape, a.dtype) for a in arrays]
+        + [pltpu.VMEM(arrays[-1].shape, F32)]
         + [pltpu.SemaphoreType.DMA((len(arrays), PARTS))] * 2,
         compiler_params=pltpu.CompilerParams(vmem_limit_bytes=60 * 1024 * 1024),
     )(*arrays)
@@ -434,7 +441,7 @@
     block = jax.ShapeDtypeStruct((rows, width), BF16)
     outs = pl.pallas_call(
         functools.partial(kernel, n_tm, n_dp, inv_count),
-        out_shape=(block, block, block, block, jax.ShapeDtypeStruct((shard, width), F32)),
+        out_shape=(block, block, block, block, jax.ShapeDtypeStruct((shard, width), BF16)),
         in_specs=[pl.BlockSpec(memory_space=pltpu.SMEM), hbm, hbm, hbm, hbm, hbm],
         out_specs=(vmem,) * 5,
         scratch_shapes=[

time: 48.9 us -> 48.3 us (0.988)
  Pallas kernels: 47.5 us -> 46.9 us
where the time goes in v3:
time: 48.3 us; the launch traced here: 48.2 us
  Pallas kernels  46.9 us (97%)
  between operations  1.29 us (3%)
    pallas_call x1, Pallas kernels, per_device(): pl.pallas_call(functools.partial(kernel, n_tm, n_dp, inv_count), out_shap...  44.1 us
    pallas_call x1, Pallas kernels, hand_over(): pl.pallas_call(functools.partial(hand_over_kernel, len(arrays)), out_shap...  2.78 us

profile of v3, /device:TPU:1, one launch (start us, length us, event | category | flops | bytes accessed | tf_op | source)
XLA Modules:
  0.0 48.2 jit_solution(15786950773179311729)
XLA Ops:
  1.3 44.1 %shard_map.101 = (bf16[256,1024]{1,0:T(8,128)(2,1)}, bf16[256,1024]{1,0:T(8,128)(2,1)}, bf16[256,1024]{1,0:T(8,128)(2,1)}, bf16[256,1024]{1,0:T(8,128)(2,1)}, bf16[256,1024]{1,0:T(8,128)(2,1)}) custom-call(s32[1]{0:T(128)S(6)} %copy.11.len_ref, bf16[256,1024]{1,0:T(8,128)(2,1)} %bitcast.8, bf16[256,1024]{1,0:T(8,128)(2,1)} %bitcast.9, ...), custom_call_target="tpu_custom_call" | custom-call | flops 4000000000 | bytes 8000000 | tf_op jit(solution)/shard_map/pallas_call | solution.py:442
  45.4 2.8 %shard_map.102 = (bf16[256,1024]{1,0:T(8,128)(2,1)}, bf16[256,1024]{1,0:T(8,128)(2,1)}, bf16[256,1024]{1,0:T(8,128)(2,1)}, bf16[256,1024]{1,0:T(8,128)(2,1)}, f32[256,1024]{1,0:T(8,128)}) custom-call(bf16[256,1024]{1,0:T(8,128)(2,1)} %get-tuple-element.15.refs_0_, bf16[256,1024]{1,0:T(8,128)(2,1)} %get-tuple-element.16.refs_1_, ...), custom_call_target="tpu_custom_call" | custom-call | tf_op jit(solution)/shard_map/pallas_call | solution.py:414

commit v4 on v3

--- a/solution.py
+++ b/solution.py
@@ -231,10 +231,11 @@
     def _(step):
         s = lax.rem(dp + n_dp - step, n_dp)
 
-        @pl.when(step < n_dp - 1)
-        def _():
-            w_copy(step).wait_recv()
-            w_forward(step).start()
+        @pl.when(step == 1)
+        def _():
+            for k in range(n_dp - 1):
+                w_copy(k).wait_recv()
+                w_forward(k).start()
 
         @pl.when(step > 0)
         def _():

time: 48.3 us -> 48.1 us (level)
  no operation moved by 1% of the time
where the time goes in v4:
time: 48.1 us; the launch traced here: 48 us
  Pallas kernels  46.7 us (97%)
  between operations  1.29 us (3%)
    pallas_call x1, Pallas kernels, per_device(): pl.pallas_call(functools.partial(kernel, n_tm, n_dp, inv_count), out_shap...  43.9 us
    pallas_call x1, Pallas kernels, hand_over(): pl.pallas_call(functools.partial(hand_over_kernel, len(arrays)), out_shap...  2.78 us

profile of v4, /device:TPU:1, one launch (start us, length us, event | category | flops | bytes accessed | tf_op | source)
XLA Modules:
  0.0 48.0 jit_solution(17432961697314176286)
XLA Ops:
  1.3 43.9 %shard_map.101 = (bf16[256,1024]{1,0:T(8,128)(2,1)}, bf16[256,1024]{1,0:T(8,128)(2,1)}, bf16[256,1024]{1,0:T(8,128)(2,1)}, bf16[256,1024]{1,0:T(8,128)(2,1)}, bf16[256,1024]{1,0:T(8,128)(2,1)}) custom-call(s32[1]{0:T(128)S(6)} %copy.11.len_ref, bf16[256,1024]{1,0:T(8,128)(2,1)} %bitcast.8, bf16[256,1024]{1,0:T(8,128)(2,1)} %bitcast.9, ...), custom_call_target="tpu_custom_call" | custom-call | flops 4000000000 | bytes 8000000 | tf_op jit(solution)/shard_map/pallas_call | solution.py:443
  45.2 2.8 %shard_map.102 = (bf16[256,1024]{1,0:T(8,128)(2,1)}, bf16[256,1024]{1,0:T(8,128)(2,1)}, bf16[256,1024]{1,0:T(8,128)(2,1)}, bf16[256,1024]{1,0:T(8,128)(2,1)}, f32[256,1024]{1,0:T(8,128)}) custom-call(bf16[256,1024]{1,0:T(8,128)(2,1)} %get-tuple-element.15.refs_0_, bf16[256,1024]{1,0:T(8,128)(2,1)} %get-tuple-element.16.refs_1_, ...), custom_call_target="tpu_custom_call" | custom-call | tf_op jit(solution)/shard_map/pallas_call | solution.py:415
